TPU v7x, 32 devices: a whole 2x2x4 slice. The times are simulated.
32 devices in a mesh: groups: 2 (over y), shard: 4 (over z), sub: 2 (over x), cores: 2 (over core).
Axes of the slice: x: 2, y: 2, z: 4, core: 2. Of those that a mesh axis runs over, the one named last changes fastest.
Arguments:
- embeddings: float32 [32768, 768], P(('groups', 'shard', 'sub', 'cores')), parts along dimension 0, may hold values from -30 to 30
- bucket_pos: int32 [32768], P(('groups', 'shard', 'sub', 'cores')), parts along dimension 0, may hold values from 0 to 16383, as said below
- tile_valid: int32 [8, 4], P(('groups', 'sub', 'cores')), parts along dimension 0, may hold values from 512 to 1024, as said below
- pair_mask: int32 [8, 4], P(('groups', 'sub', 'cores')), parts along dimension 0, may hold values 0 or 1
Outputs:
- neighbour_sums: float32 [8, 4096, 768], P(('groups', 'sub', 'cores'), 'shard'), parts along dimension 0
There are 2 independent parts, one for each index of `groups`. A program takes and returns all parts, laid end to end along the dimension named above; each array names one. Nothing has to cross between parts.
Inputs may be any that keep to these rules, and one draw needn't show every extreme that they name: `bucket_pos`: A permutation giving every ingest row its own place in bucket order. Of the 1024 rows of one ingest block (one device's rows), at most 128 go to any one tile, and every block sends exactly 128 rows to some tile. `tile_valid`: rows of a tile past its count are padding.
All inputs are finite; a program needn't handle non-finite values. No bound on the sum of `pair_mask` on one device may be relied on, other than what follows from the above.
Results may differ from a plain program's by a relative error of at most 0.0023.
Values may be sent and summed in bfloat16 or wider, within the bound.
A program may use at most 64 MiB of HBM per device.

v0:
```python
import jax
import jax.numpy as jnp
from jax import lax
from jax.sharding import PartitionSpec as P

D = 768


beta = 8.0
epsilon = 1e-06


def passed_along(value, axis, steps):
    count = lax.axis_size(axis)
    first, last = (max(0, -steps), min(count, count - steps))
    return lax.ppermute(value, axis, [(source, source + steps) for source in range(first, last)])


def row_scale(block):
    return lax.rsqrt(jnp.mean(jnp.square(block.astype(jnp.float32)), axis=-1) + epsilon)


def kernel_block(query, query_scale, keys, key_scale):
    gram = lax.dot_general(
        query, keys, (((1,), (1,)), ((), ())), preferred_element_type=jnp.float32
    )
    return jnp.exp(beta * (query_scale[:, None] * key_scale[None, :] * gram) / D)


def pick_entry(values, index):
    return jnp.sum(jnp.where(jnp.arange(values.shape[0], dtype=jnp.int32) == index, values, 0))


def forward_pair(own_tile, own_scale, neighbour, neighbour_valid):
    weights = (
        kernel_block(own_tile, own_scale, neighbour, row_scale(neighbour))
        * neighbour_valid[None, :]
    )
    numer = jnp.dot(weights.astype(jnp.bfloat16), neighbour, preferred_element_type=jnp.float32)
    return (numer, jnp.sum(weights, axis=1))


def skipped_pair(own_tile, own_scale, neighbour, neighbour_valid):
    return (jnp.zeros(own_tile.shape, jnp.float32), jnp.zeros((own_tile.shape[0],), jnp.float32))


def body(embeddings, bucket_pos, tile_valid, pair_mask):
    shards = lax.axis_size("shard")
    band_count = lax.axis_size("sub") * lax.axis_size("cores")
    owners = shards * band_count
    tile_rows = embeddings.shape[0]
    width = embeddings.shape[1]
    capacity = 2 * tile_rows // owners
    lowered = embeddings.astype(jnp.bfloat16)
    target_band = bucket_pos // (shards * tile_rows)
    target_shard = bucket_pos // tile_rows % shards
    target_row = bucket_pos % tile_rows
    owner = target_shard * band_count + target_band
    onehot = (owner[:, None] == jnp.arange(owners, dtype=jnp.int32)[None, :]).astype(jnp.int32)
    rank_in = jnp.sum(jnp.cumsum(onehot, axis=0) * onehot, axis=1) - 1
    slot_index = owner * capacity + rank_in
    outgoing = jnp.zeros((owners * capacity, width), jnp.bfloat16).at[slot_index].set(lowered)
    addresses = jnp.full((owners * capacity,), tile_rows, jnp.int32).at[slot_index].set(target_row)
    incoming, arrived = (
        lax.all_to_all(
            lax.all_to_all(
                outgoing.reshape(shards, band_count, capacity, width),
                "shard",
                split_axis=0,
                concat_axis=0,
                tiled=True,
            ),
            ("sub", "cores"),
            split_axis=1,
            concat_axis=1,
            tiled=True,
        ),
        lax.all_to_all(
            lax.all_to_all(
                addresses.reshape(shards, band_count, capacity),
                "shard",
                split_axis=0,
                concat_axis=0,
                tiled=True,
            ),
            ("sub", "cores"),
            split_axis=1,
            concat_axis=1,
            tiled=True,
        ),
    )
    own_tile = (
        jnp.zeros((tile_rows, width), jnp.bfloat16)
        .at[arrived.reshape(-1)]
        .set(incoming.reshape(-1, width), mode="drop")
    )
    own_scale = row_scale(own_tile)
    my_shard = lax.axis_index("shard")
    counts = tile_valid[0]
    masks = pair_mask[0]
    row_index = jnp.arange(tile_rows, dtype=jnp.int32)
    own_valid = (row_index < pick_entry(counts, my_shard)).astype(jnp.float32)
    kernel = kernel_block(own_tile, own_scale, own_tile, own_scale)
    kernel = jnp.where(row_index[:, None] == row_index[None, :], 0.0, kernel) * own_valid[None, :]
    numer = jnp.dot(kernel.astype(jnp.bfloat16), own_tile, preferred_element_type=jnp.float32)
    denom = jnp.sum(kernel, axis=1)
    for offset in (1, -1):
        neighbour = passed_along(own_tile, "shard", offset)
        source = my_shard - offset
        lower = jnp.minimum(my_shard, source)
        pair_live = (source >= 0) & (source < shards) & (pick_entry(masks, lower) == 1)
        neighbour_valid = (row_index < pick_entry(counts, source)).astype(jnp.float32)
        extra_numer, extra_denom = lax.cond(
            pair_live, forward_pair, skipped_pair, own_tile, own_scale, neighbour, neighbour_valid
        )
        numer = numer + extra_numer
        denom = denom + extra_denom
    result = jnp.where(own_valid[:, None] > 0, numer / denom[:, None], 0.0)
    return result.reshape(1, tile_rows, width)


def solution(mesh):
    placed = (
        P(("groups", "shard", "sub", "cores"), None),
        P(("groups", "shard", "sub", "cores")),
        P(("groups", "sub", "cores"), None),
        P(("groups", "sub", "cores"), None),
    )
    return jax.shard_map(
        body,
        mesh=mesh,
        in_specs=placed,
        out_specs=P(("groups", "sub", "cores"), "shard", None),
        check_vma=False,
    )
```

profile of v0, /device:TPU:14, one launch (start us, length us, event | category | flops | bytes accessed | tf_op | source)
XLA Modules:
  0.0 217.8 jit_solution(5871489498932138251)
XLA Ops:
  0.7 4.5 %reduce-window.6 = s32[16,8,128]{2,1,0:T(8,128)S(1)} reduce-window(s32[16,8,128]{2,1,0:T(8,128)S(1)} %fusion.34, s32[]{:T(128)} %constant.103.clone.1), window={size=1x1x128 pad=0_0x0_0x127_0}, to_apply=%region_1.2 | reduce-window | flops 2080768 | bytes 131076 | tf_op jit(solution)/shard_map/reduce-window
  5.7 4.9 %scatter_custom_fusion = s32[2048]{0:T(1024)} fusion(s32[1024]{0:T(1024)S(1)} %compare_select_fusion.1, s32[1024]{0:T(1024)S(1)} %get-tuple-element.46, s32[]{:T(128)} %constant.106.clone.1), kind=kCustom, calls=%fused_computation.71 | custom fusion | bytes 8196 | tf_op jit(solution)/shard_map/scatter | solution.py:63
  10.6 5.3 %all-to-all-start = ((s32[4,4,128]{2,1,0:T(4,128)}), s32[4,4,128]{2,1,0:T(4,128)S(1)}, u32[]{:S(2)}, u32[]{:S(2)}) async-start(s32[4,4,128]{2,1,0:T(4,128)} %bitcast.4), calls=%async_computation | async-start | bytes 16384 | tf_op jit(solution)/shard_map/all_to_all | solution.py:79
  15.9 8.2 %scatter_custom_fusion.1 = bf16[2048,768]{1,0:T(8,128)(2,1)} fusion(s32[1024]{0:T(1024)S(1)} %compare_select_fusion.1, f32[1024,768]{1,0:T(8,128)} %param.8, bf16[]{:T(256)} %constant.105.clone.1), kind=kCustom, calls=%fused_computation.37 | custom fusion | flops 786432 | bytes 6291458 | tf_op jit(solution)/shard_map/scatter | solution.py:62
  24.1 5.1 %all-to-all-start.2 = ((bf16[4,4,128,768]{3,2,1,0:T(8,128)(2,1)}), bf16[4,4,128,768]{3,2,1,0:T(8,128)(2,1)S(1)}, u32[]{:S(2)}, u32[]{:S(2)}) async-start(bf16[4,4,128,768]{3,2,1,0:T(8,128)(2,1)} %bitcast.41), calls=%async_computation.2 | async-start | bytes 6291456 | tf_op jit(solution)/shard_map/all_to_all | solution.py:66
  29.8 66.2 %all-to-all-done.2 = bf16[4,4,128,768]{3,2,1,0:T(8,128)(2,1)S(1)} async-done(((bf16[4,4,128,768]{3,2,1,0:T(8,128)(2,1)}), bf16[4,4,128,768]{3,2,1,0:T(8,128)(2,1)S(1)}, u32[]{:S(2)}, u32[]{:S(2)}) %all-to-all-start.2) | async-done | bytes 3145760 | tf_op jit(solution)/shard_map/all_to_all | solution.py:66
  96.0 3.8 %all-to-all-start.1 = ((s32[4,4,128]{2,0,1:T(4,128)}), s32[4,4,128]{2,0,1:T(4,128)S(1)}, u32[]{:S(2)}, u32[]{:S(2)}) async-start(s32[4,4,128]{2,0,1:T(4,128)} %copy.20), calls=%async_computation.1 | async-start | bytes 16384 | tf_op jit(solution)/shard_map/all_to_all | solution.py:78
  99.7 1.9 copy.22
  101.6 5.6 %all-to-all-start.3 = ((bf16[4,4,128,768]{3,2,0,1:T(8,128)(2,1)}), bf16[4,4,128,768]{3,2,0,1:T(8,128)(2,1)S(1)}, u32[]{:S(2)}, u32[]{:S(2)}) async-start(bf16[4,4,128,768]{3,2,0,1:T(8,128)(2,1)} %copy.22), calls=%async_computation.3 | async-start | bytes 6291456 | tf_op jit(solution)/shard_map/all_to_all | solution.py:65
  111.8 30.7 %all-to-all-done.3 = bf16[4,4,128,768]{3,2,0,1:T(8,128)(2,1)S(1)} async-done(((bf16[4,4,128,768]{3,2,0,1:T(8,128)(2,1)}), bf16[4,4,128,768]{3,2,0,1:T(8,128)(2,1)S(1)}, u32[]{:S(2)}, u32[]{:S(2)}) %all-to-all-start.3) | async-done | bytes 3145760 | tf_op jit(solution)/shard_map/all_to_all | solution.py:65
  142.5 1.9 copy.23
  144.4 11.4 %scatter_custom_fusion.2 = bf16[1024,768]{1,0:T(8,128)(2,1)} fusion(s32[2048]{0:T(1024)S(1)} %bitcast.47, bf16[2048,768]{1,0:T(8,128)(2,1)} %bitcast.42, bf16[]{:T(256)} %constant.105.clone.1), kind=kCustom, calls=%fused_computation.40 | custom fusion | bytes 1573376 | tf_op jit(solution)/shard_map/scatter | solution.py:95
  155.8 5.2 %collective-permute-start.1 = (bf16[1024,768]{1,0:T(8,128)(2,1)}, bf16[1024,768]{1,0:T(8,128)(2,1)S(1)}, u32[]{:S(2)}, u32[]{:S(2)}) collective-permute-start(bf16[1024,768]{1,0:T(8,128)(2,1)} %scatter_custom_fusion.2), channel_id=1, source_target_pairs={{4,0},{8,4},{12,8},{5,1},{9,5},{13,9},{6,2},{10,6},{14,10},{7,3},{... | collective-permute-start | bytes 4718600 | tf_op jit(solution)/shard_map/ppermute | solution.py:16
  161.0 2.1 collective-permute-start
  164.9 4.8 %fusion.18 = (f32[1024]{0:T(1024)S(1)}, f32[1024,1024]{0,1:T(8,128)S(1)}) fusion(f32[1024]{0:T(1024)S(1)} %get-tuple-element.50, f32[1024]{0:T(1024)S(1)} %add_rsqrt_fusion.2, bf16[1024,768]{1,0:T(8,128)(2,1)} %scatter_custom_fusion.2), kind=kOutput, calls=%fused_computation.29 | convolution fusion | flops 1617951744 | bytes 5779456 | tf_op jit(solution)/shard_map/dot_general | solution.py:24
  169.7 5.6 %fusion.20 = f32[1024,768]{1,0:T(8,128)} fusion(bf16[1024,768]{1,0:T(8,128)(2,1)} %scatter_custom_fusion.2, f32[1024,1024]{0,1:T(8,128)S(1)} %get-tuple-element.49, f32[1024]{0:T(1024)S(1)} %get-tuple-element.50, f32[1024]{0:T(1024)S(1)} %add_rsqrt_fusion.2), kind=kOutput, calls=%fused_computation.31 | convolution fusion | flops 1617952768 | bytes 8921088 | tf_op jit(solution)/shard_map/dot_general | solution.py:105
  175.3 19.7 %collective-permute-done.1 = bf16[1024,768]{1,0:T(8,128)(2,1)S(1)} collective-permute-done((bf16[1024,768]{1,0:T(8,128)(2,1)}, bf16[1024,768]{1,0:T(8,128)(2,1)S(1)}, u32[]{:S(2)}, u32[]{:S(2)}) %collective-permute-start.1) | collective-permute-done | bytes 1572896 | tf_op jit(solution)/shard_map/ppermute | solution.py:16
  195.0 6.5 %conditional.3 = (f32[1024,768]{1,0:T(8,128)S(1)}, f32[1024]{0:T(1024)S(1)}) conditional(s32[]{:T(128)} %convert_element_type.56, () %tuple.23, (f32[1024]{0:T(1024)S(1)}, bf16[1024,768]{1,0:T(8,128)(2,1)S(1)}, bf16[1024,768]{1,0:T(8,128)(2,1)}, f32[1024]{0:T(1024)S(1)}) %tuple.24), branch_computations={%region_16.17_spmd, %region_17.20_spmd} | conditional | flops 3234070528 | bytes 17866768 | solution.py:113
  195.4 3.5 %fusion.9 = (f32[1024]{0:T(1024)S(1)}, f32[1024,1024]{0,1:T(8,128)S(1)}) fusion(f32[1024]{0:T(1024)S(1)} %get-tuple-element.28, f32[1024]{0:T(1024)S(1)} %add_rsqrt_fusion.1, f32[1024]{0:T(1024)S(1)} %get-tuple-element.25, bf16[1024,768]{1,0:T(8,128)(2,1)} %get-tuple-element.27, bf16[1024,768]{1,0:T(8,128)(2,1)S(1)} %get-tuple-element.26), kind=kOutput, calls=%fused_computation.16 | convolution fusion | flops 1615854592 | bytes 7356416 | tf_op jit(solution)/shard_map/cond/branch_1_fun/dot_general | solution.py:24
  198.9 2.5 %fusion.11 = f32[1024,768]{1,0:T(8,128)S(1)} fusion(bf16[1024,768]{1,0:T(8,128)(2,1)S(1)} %get-tuple-element.26, f32[1024,1024]{0,1:T(8,128)S(1)} %get-tuple-element.45, f32[1024]{0:T(1024)S(1)} %get-tuple-element.28, f32[1024]{0:T(1024)S(1)} %add_rsqrt_fusion.1, f32[1024]{0:T(1024)S(1)} %get-tuple-element.25), kind=kOutput, calls=%fused_computation.18 | convolution fusion | flops 1615855616 | bytes 8925184 | tf_op jit(solution)/shard_map/cond/branch_1_fun/dot_general | solution.py:39
  201.5 11.9 %conditional.2 = (f32[1024,768]{1,0:T(8,128)}, f32[1024]{0:T(1024)S(1)}) conditional(s32[]{:T(128)} %convert_element_type.54, () %tuple.21, (f32[1024]{0:T(1024)S(1)}, bf16[1024,768]{1,0:T(8,128)(2,1)}, bf16[1024,768]{1,0:T(8,128)(2,1)}, f32[1024]{0:T(1024)S(1)}) %tuple.22), branch_computations={%region_10.11_spmd, %region_11.14_spmd} | conditional | flops 3234070528 | bytes 17866768 | solution.py:113
  203.6 4.3 %fusion = (f32[1024]{0:T(1024)S(1)}, f32[1024,1024]{0,1:T(8,128)S(1)}) fusion(f32[1024]{0:T(1024)S(1)} %get-tuple-element.24, f32[1024]{0:T(1024)S(1)} %add_rsqrt_fusion, f32[1024]{0:T(1024)S(1)} %get-tuple-element.21, bf16[1024,768]{1,0:T(8,128)(2,1)} %get-tuple-element.23, bf16[1024,768]{1,0:T(8,128)(2,1)} %get-tuple-element.22), kind=kOutput, calls=%fused_computation.5 | convolution fusion | flops 1615854592 | bytes 7356416 | tf_op jit(solution)/shard_map/cond/branch_1_fun/dot_general | solution.py:24
  207.8 5.6 %fusion.2 = f32[1024,768]{1,0:T(8,128)} fusion(bf16[1024,768]{1,0:T(8,128)(2,1)} %get-tuple-element.22, f32[1024,1024]{0,1:T(8,128)S(1)} %get-tuple-element.43, f32[1024]{0:T(1024)S(1)} %get-tuple-element.24, f32[1024]{0:T(1024)S(1)} %add_rsqrt_fusion, f32[1024]{0:T(1024)S(1)} %get-tuple-element.21), kind=kOutput, calls=%fused_computation.7 | convolution fusion | flops 1615855616 | bytes 8925184 | tf_op jit(solution)/shard_map/cond/branch_1_fun/dot_general | solution.py:39
  213.4 4.4 %select_bitcast_fusion = f32[1,1024,768]{2,1,0:T(8,128)} fusion(f32[1024,768]{1,0:T(8,128)S(1)} %get-tuple-element.34, f32[1024,768]{1,0:T(8,128)} %fusion.20, f32[1024,768]{1,0:T(8,128)} %get-tuple-element.33, f32[1024]{0:T(1024)S(1)} %add_add_fusion, pred[1024]{0:T(1024)(128)(4,1)S(1)} %get-tuple-element.51), kind=kLoop, calls=%fused_computation.27 | loop fusion | flops 3145728 | bytes 12588032 | tf_op jit(solution)/shard_map/reshape | solution.py:119
  (32 shorter events, 9.0 us)
Async XLA Ops:
  10.6 13.5 %all-to-all-start = ((s32[4,4,128]{2,1,0:T(4,128)}), s32[4,4,128]{2,1,0:T(4,128)S(1)}, u32[]{:S(2)}, u32[]{:S(2)}) async-start(s32[4,4,128]{2,1,0:T(4,128)} %bitcast.4), calls=%async_computation | async-start | bytes 16384 | tf_op jit(solution)/shard_map/all_to_all | solution.py:79
  24.1 71.9 %all-to-all-start.2 = ((bf16[4,4,128,768]{3,2,1,0:T(8,128)(2,1)}), bf16[4,4,128,768]{3,2,1,0:T(8,128)(2,1)S(1)}, u32[]{:S(2)}, u32[]{:S(2)}) async-start(bf16[4,4,128,768]{3,2,1,0:T(8,128)(2,1)} %bitcast.41), calls=%async_computation.2 | async-start | bytes 6291456 | tf_op jit(solution)/shard_map/all_to_all | solution.py:66
  96.0 5.6 %all-to-all-start.1 = ((s32[4,4,128]{2,0,1:T(4,128)}), s32[4,4,128]{2,0,1:T(4,128)S(1)}, u32[]{:S(2)}, u32[]{:S(2)}) async-start(s32[4,4,128]{2,0,1:T(4,128)} %copy.20), calls=%async_computation.1 | async-start | bytes 16384 | tf_op jit(solution)/shard_map/all_to_all | solution.py:78
  101.6 5.6 %copy-start = (s32[1,4]{1,0:T(1,128)S(1)}, s32[1,4]{1,0:T(1,128)}, u32[]{:S(2)}) copy-start(s32[1,4]{1,0:T(1,128)} %param.11) | copy-start | bytes 52
  101.6 7.6 %copy-start.1 = (s32[1,4]{1,0:T(1,128)S(1)}, s32[1,4]{1,0:T(1,128)}, u32[]{:S(2)}) copy-start(s32[1,4]{1,0:T(1,128)} %param.10) | copy-start | bytes 52
  101.6 40.9 %all-to-all-start.3 = ((bf16[4,4,128,768]{3,2,0,1:T(8,128)(2,1)}), bf16[4,4,128,768]{3,2,0,1:T(8,128)(2,1)S(1)}, u32[]{:S(2)}, u32[]{:S(2)}) async-start(bf16[4,4,128,768]{3,2,0,1:T(8,128)(2,1)} %copy.22), calls=%async_computation.3 | async-start | bytes 6291456 | tf_op jit(solution)/shard_map/all_to_all | solution.py:65
  155.8 39.2 %collective-permute-start.1 = (bf16[1024,768]{1,0:T(8,128)(2,1)}, bf16[1024,768]{1,0:T(8,128)(2,1)S(1)}, u32[]{:S(2)}, u32[]{:S(2)}) collective-permute-start(bf16[1024,768]{1,0:T(8,128)(2,1)} %scatter_custom_fusion.2), channel_id=1, source_target_pairs={{4,0},{8,4},{12,8},{5,1},{9,5},{13,9},{6,2},{10,6},{14,10},{7,3},{... | collective-permute-start | bytes 4718600 | tf_op jit(solution)/shard_map/ppermute | solution.py:16
  161.0 40.5 %collective-permute-start = (bf16[1024,768]{1,0:T(8,128)(2,1)}, bf16[1024,768]{1,0:T(8,128)(2,1)}, u32[]{:S(2)}, u32[]{:S(2)}) collective-permute-start(bf16[1024,768]{1,0:T(8,128)(2,1)} %scatter_custom_fusion.2), channel_id=1, source_target_pairs={{0,4},{4,8},{8,12},{1,5},{5,9},{9,13},{2,6},{6,10},{10,14},{3,7},{... | collective-permute-start | bytes 4718600 | tf_op jit(solution)/shard_map/ppermute | solution.py:16
where the time goes:
time: 219 us; the launch traced here: 218 us
  waiting for transfers between devices  117 us (53%)
  starting transfers between devices  27 us (12%)
  matrix products  26.4 us (12%)
  other arithmetic  25.2 us (12%)
  local copies, waits for them, and re-layouts  21 us (10%)
    all_to_all x1, waiting for transfers between devices, body(): lax.all_to_all(outgoing.reshape(shards, band_count, capacity, width), 'sh...  66.2 us
    all_to_all x1, waiting for transfers between devices, body(): lax.all_to_all(lax.all_to_all(outgoing.reshape(shards, band_count, capaci...  30.7 us
    ppermute x2, waiting for transfers between devices, passed_along(): lax.ppermute(value, axis, [(source, source + steps) for source in range(f...  19.7 us
    dot_general x3, matrix products, kernel_block(): lax.dot_general(query, keys, (((1,), (1,)), ((), ())), preferred_element_...  12.6 us
    scatter x1, local copies, waits for them, and re-layouts, body(): own_tile = jnp.zeros((tile_rows, width), jnp.bfloat16).at[arrived.reshape...  11.4 us
    scatter x1, other arithmetic, body(): jnp.zeros((owners * capacity, width), jnp.bfloat16).at[slot_index]  8.16 us
    dot_general x2, matrix products, forward_pair(): jnp.dot(weights.astype(jnp.bfloat16), neighbour, preferred_element_type=j...  8.12 us
    ppermute x2, starting transfers between devices, passed_along(): lax.ppermute(value, axis, [(source, source + steps) for source in range(f...  7.27 us
  transfers between devices with their start and end apart: 6, of which 3 were waited for; matrix products, arithmetic and copies ran while one was open for 15% of the time, Pallas kernels for 0%

commit v1 on v0

v1 whole, which is shorter than its diff:
```python
import functools

import jax
import jax.numpy as jnp
from jax import lax
from jax.experimental import pallas as pl
from jax.experimental.pallas import tpu as pltpu
from jax.sharding import PartitionSpec as P

beta = 8.0
epsilon = 1e-06
LOG2E = 1.4426950408889634
MESH = pl.DeviceIdType.MESH
ROWS = 256


def far_first(shards):
    return sorted(range(shards), key=lambda d: -min(d, shards - d))


def dot_t(a, b):
    return lax.dot_general(a, b, (((1,), (1,)), ((), ())), preferred_element_type=jnp.float32)


def kernel(
    shards, subs, cores, cap,
    emb, pos, counts, masks, out,
    low, outgoing, incoming, addr_out, addr_in, acc, own, scale_col, scale_row, near, near_scale,
    denom,
    send, recv, addr_send, addr_recv, near_send, near_recv, ns_send, ns_recv,
):
    tile, width = emb.shape
    bands = subs * cores
    owners = shards * bands
    blocks = tile // ROWS
    slots = bands * cap
    group = lax.axis_index("groups")
    shard = lax.axis_index("shard")
    band = lax.axis_index("sub") * cores + lax.axis_index("cores")
    me = shard * bands + band

    def place(z, b):
        return (group, z, b // cores, b % cores)

    barrier = pltpu.get_barrier_semaphore()

    @pl.loop(1, owners)
    def _(step):
        peer = (me + step) % owners
        pl.semaphore_signal(
            barrier, inc=1, device_id=place(peer // bands, peer % bands), device_id_type=MESH
        )

    low[...] = emb[...].astype(jnp.bfloat16)
    where = pos[...]
    owner = where // tile % shards * bands + where // (shards * tile)
    row = where % tile + 1
    chosen = lax.broadcasted_iota(jnp.int32, (owners, tile), 0) == owner
    upto = lax.broadcasted_iota(jnp.int32, (tile, tile), 0) <= lax.broadcasted_iota(
        jnp.int32, (tile, tile), 1
    )
    rank = jnp.dot(
        jnp.where(chosen, 1.0, 0.0).astype(jnp.bfloat16),
        jnp.where(upto, 1.0, 0.0).astype(jnp.bfloat16),
        preferred_element_type=jnp.float32,
    )
    rank = jnp.sum(jnp.where(chosen, rank, 0.0), axis=0, keepdims=True).astype(jnp.int32) - 1
    slot = owner * cap + rank
    which = lax.broadcasted_iota(jnp.int32, (16, tile), 0)
    parts = jnp.where(which == 0, row // 32, jnp.where(which == 1, row % 32, 0))
    parts = parts.astype(jnp.float32).astype(jnp.bfloat16)

    def data_copy(source, target, z, b):
        return pltpu.make_async_remote_copy(
            src_ref=outgoing.at[target], dst_ref=incoming.at[source],
            send_sem=send.at[target], recv_sem=recv.at[source],
            device_id=place(z, b), device_id_type=MESH,
        )

    def addr_copy(source, target, z, b):
        return pltpu.make_async_remote_copy(
            src_ref=addr_out.at[target], dst_ref=addr_in.at[source],
            send_sem=addr_send.at[target], recv_sem=addr_recv.at[source],
            device_id=place(z, b), device_id_type=MESH,
        )

    order = far_first(shards)
    for step, dz in enumerate(order):
        z = (shard + dz) % shards
        pick = lax.broadcasted_iota(jnp.int32, (slots, tile), 0) + z * slots == slot
        pick = jnp.where(pick, 1.0, 0.0).astype(jnp.bfloat16)
        packed = jnp.dot(pick, low[...], preferred_element_type=jnp.float32)
        outgoing[pl.ds(z * bands, bands)] = packed.astype(jnp.bfloat16).reshape(bands, cap, width)
        address = dot_t(parts, pick)
        address = (32.0 * address[0:1] + address[1:2]).astype(jnp.int32) - 1
        for b in range(bands):
            addr_out[z * bands + b] = address[:, b * cap : (b + 1) * cap]
        if step == 0:
            pl.semaphore_wait(barrier, owners - 1)
        for j in range(1 if dz == 0 else 0, bands):
            b = (band + j) % bands
            addr_copy(me, z * bands + b, z, b).start()
            data_copy(me, z * bands + b, z, b).start()
        if dz == 0:
            incoming[pl.ds(me, 1)] = outgoing[pl.ds(me, 1)]
            addr_in[pl.ds(me, 1)] = addr_out[pl.ds(me, 1)]

    def near_copy(block, side):
        z = (shard + (shards - 1 if side else 1)) % shards
        rows = pl.ds(pl.multiple_of(block * ROWS, ROWS), ROWS)
        return pltpu.make_async_remote_copy(
            src_ref=own.at[rows], dst_ref=near.at[side, rows],
            send_sem=near_send.at[side, block], recv_sem=near_recv.at[side, block],
            device_id=place(z, band), device_id_type=MESH,
        )

    def scale_copy(block, side):
        z = (shard + (shards - 1 if side else 1)) % shards
        return pltpu.make_async_remote_copy(
            src_ref=scale_row.at[block], dst_ref=near_scale.at[side, block],
            send_sem=ns_send.at[side, block], recv_sem=ns_recv.at[side, block],
            device_id=place(z, band), device_id_type=MESH,
        )

    for step, dz in enumerate(order):
        z = (shard + shards - dz) % shards
        for j in range(1 if dz == 0 else 0, bands):
            b = (band + bands - j) % bands
            addr_copy(z * bands + b, z * bands + b, z, b).wait_recv()
            data_copy(z * bands + b, z * bands + b, z, b).wait_recv()
        address = jnp.concatenate([addr_in[z * bands + b] for b in range(bands)], axis=1)

        @pl.loop(0, blocks)
        def _(block):
            rows = pl.ds(pl.multiple_of(block * ROWS, ROWS), ROWS)
            put = lax.broadcasted_iota(jnp.int32, (ROWS, slots), 0) + block * ROWS == address
            put = jnp.where(put, 1.0, 0.0).astype(jnp.bfloat16)
            arrived = incoming[pl.ds(z * bands, bands)].reshape(slots, width)
            total = jnp.dot(put, arrived, preferred_element_type=jnp.float32)
            if step > 0:
                total = total + acc[rows]
            if step < shards - 1:
                acc[rows] = total
            else:
                own[rows] = total.astype(jnp.bfloat16)
                scale = lax.rsqrt(jnp.mean(jnp.square(total), axis=1, keepdims=True) + epsilon)
                scale = jnp.broadcast_to(scale, (ROWS, 128))
                scale_col[rows] = scale
                scale_row[block] = jnp.transpose(scale)[0:1]

                @pl.when(shard < shards - 1)
                def _():
                    scale_copy(block, 0).start()
                    near_copy(block, 0).start()

                @pl.when(shard > 0)
                def _():
                    scale_copy(block, 1).start()
                    near_copy(block, 1).start()

    def add_keys(keys, key_scale, key_weight, first_key, first):
        @pl.loop(0, blocks)
        def _(block):
            rows = pl.ds(pl.multiple_of(block * ROWS, ROWS), ROWS)
            gram = dot_t(own[rows], keys)
            weight = jnp.exp2(
                gram * (scale_col[rows, 0:1] * (beta * LOG2E / width)) * key_scale
            ) * key_weight
            if first_key is not None:
                at = lax.broadcasted_iota(jnp.int32, weight.shape, 0) + block * ROWS
                key = lax.broadcasted_iota(jnp.int32, weight.shape, 1) + first_key
                weight = jnp.where(at == key, 0.0, weight)
            numer = jnp.dot(weight.astype(jnp.bfloat16), keys, preferred_element_type=jnp.float32)
            total = weight[:, 0:128]
            for k in range(128, weight.shape[1], 128):
                total = total + weight[:, k : k + 128]
            if first:
                acc[rows] = numer
                denom[rows] = total
            else:
                acc[rows] += numer
                denom[rows] += total

    lane = lax.broadcasted_iota(jnp.int32, (1, ROWS), 1)

    def counted(block, count):
        return jnp.where(lane + block * ROWS < count, 1.0, 0.0)

    own_count = counts[0, shard]
    for block in range(blocks):
        add_keys(
            own[block * ROWS : (block + 1) * ROWS], scale_row[block], counted(block, own_count),
            block * ROWS, block == 0,
        )

    before, after = (shard + shards - 1) % shards, (shard + 1) % shards
    sides = (
        (shard > 0, counts[0, before], masks[0, before]),
        (shard < shards - 1, counts[0, after], masks[0, shard]),
    )
    for block in range(blocks):
        for side, (there, count, live) in enumerate(sides):

            @pl.when(there)
            def _():
                scale_copy(block, side).wait_recv()
                near_copy(block, side).wait_recv()
                gate = counted(block, jnp.where(live == 1, count, 0))
                add_keys(
                    near[side, block * ROWS : (block + 1) * ROWS], near_scale[side, block], gate,
                    None, False,
                )

    @pl.loop(0, blocks)
    def _(block):
        rows = pl.ds(pl.multiple_of(block * ROWS, ROWS), ROWS)
        total = jnp.sum(denom[rows], axis=1, keepdims=True)
        valid = lax.broadcasted_iota(jnp.int32, (ROWS, 1), 0) + block * ROWS < own_count
        out[rows] = jnp.where(valid, acc[rows] / total, 0.0)

    for dz in order:
        z = (shard + dz) % shards
        for j in range(1 if dz == 0 else 0, bands):
            b = (band + j) % bands
            addr_copy(me, z * bands + b, z, b).wait_send()
            data_copy(me, z * bands + b, z, b).wait_send()
    for side, there in enumerate((shard < shards - 1, shard > 0)):

        @pl.when(there)
        def _():
            for block in range(blocks):
                scale_copy(block, side).wait_send()
                near_copy(block, side).wait_send()


def body(embeddings, bucket_pos, tile_valid, pair_mask):
    shards, subs, cores = (lax.axis_size(a) for a in ("shard", "sub", "cores"))
    owners = shards * subs * cores
    tile, width = embeddings.shape
    cap = 2 * tile // owners
    blocks = tile // ROWS
    vmem = pl.BlockSpec(memory_space=pltpu.VMEM)
    smem = pl.BlockSpec(memory_space=pltpu.SMEM)
    dma = pltpu.SemaphoreType.DMA
    bf16, f32 = jnp.bfloat16, jnp.float32
    result = pl.pallas_call(
        functools.partial(kernel, shards, subs, cores, cap),
        out_shape=jax.ShapeDtypeStruct((tile, width), f32),
        in_specs=[vmem, vmem, smem, smem],
        out_specs=vmem,
        scratch_shapes=[
            pltpu.VMEM((tile, width), bf16),
            pltpu.VMEM((owners, cap, width), bf16),
            pltpu.VMEM((owners, cap, width), bf16),
            pltpu.VMEM((owners, 1, cap), jnp.int32),
            pltpu.VMEM((owners, 1, cap), jnp.int32),
            pltpu.VMEM((tile, width), f32),
            pltpu.VMEM((tile, width), bf16),
            pltpu.VMEM((tile, 128), f32),
            pltpu.VMEM((blocks, 1, ROWS), f32),
            pltpu.VMEM((2, tile, width), bf16),
            pltpu.VMEM((2, blocks, 1, ROWS), f32),
            pltpu.VMEM((tile, 128), f32),
            dma((owners,)), dma((owners,)), dma((owners,)), dma((owners,)),
            dma((2, blocks)), dma((2, blocks)), dma((2, blocks)), dma((2, blocks)),
        ],
        compiler_params=pltpu.CompilerParams(
            collective_id=0, has_side_effects=True, vmem_limit_bytes=48 * 1024 * 1024
        ),
        cost_estimate=pl.CostEstimate(
            flops=20 * tile * tile * width, bytes_accessed=8 * tile * width,
            transcendentals=3 * tile * tile,
        ),
    )(embeddings, bucket_pos.reshape(1, tile), tile_valid, pair_mask)
    return result.reshape(1, tile, width)


def solution(mesh):
    placed = (
        P(("groups", "shard", "sub", "cores"), None),
        P(("groups", "shard", "sub", "cores")),
        P(("groups", "sub", "cores"), None),
        P(("groups", "sub", "cores"), None),
    )
    return jax.shard_map(
        body,
        mesh=mesh,
        in_specs=placed,
        out_specs=P(("groups", "sub", "cores"), "shard", None),
        check_vma=False,
    )
```

time: 219 us -> 123 us (0.56)
  Pallas kernels: 0 us -> 118 us
  waiting for transfers between devices: 117 us -> 0 us
  starting transfers between devices: 27 us -> 0 us
  matrix products: 26.4 us -> 0 us
  other arithmetic: 25.2 us -> 0 us
  local copies, waits for them, and re-layouts: 21 us -> 3.66 us
    pallas_call x0 -> x1, Pallas kernels: none -> 118 us  [body(): pl.pallas_call(functools.partial(kernel, shards, subs, cores, cap), out_s...]
    all_to_all x4 -> x0, waiting for transfers between devices: 96.9 us -> none  [the longest x1 66.2 us: body(): lax.all_to_all(outgoing.reshape(shards, band_count, capacity, width), 'sh...]
    dot_general x6 -> x0, matrix products: 26.4 us -> none  [the longest x3 12.6 us: kernel_block(): lax.dot_general(query, keys, (((1,), (1,)), ((), ())), preferred_element_...]
    all_to_all x4 -> x0, starting transfers between devices: 19.8 us -> none  [the longest x1 5.59 us: body(): lax.all_to_all(lax.all_to_all(outgoing.reshape(shards, band_count, capaci...]
    ppermute x2 -> x0, waiting for transfers between devices: 19.7 us -> none  [passed_along(): lax.ppermute(value, axis, [(source, source + steps) for source in range(f...]
    scatter x2 -> x0, local copies, waits for them, and re-layouts: 16.3 us -> none  [the longest x1 11.4 us: body(): own_tile = jnp.zeros((tile_rows, width), jnp.bfloat16).at[arrived.reshape...]
    scatter x1 -> x0, other arithmetic: 8.16 us -> none  [body(): jnp.zeros((owners * capacity, width), jnp.bfloat16).at[slot_index]]
    ppermute x2 -> x0, starting transfers between devices: 7.27 us -> none  [passed_along(): lax.ppermute(value, axis, [(source, source + steps) for source in range(f...]
  transfers between devices with their start and end apart: 6 -> 0, of which waited for: 3 -> 0; matrix products, arithmetic and copies ran while one was open for 15% -> 0% of each run, Pallas kernels for 0% -> 0%
where the time goes in v1:
time: 123 us; the launch traced here: 122 us
  Pallas kernels  118 us (96%)
  local copies, waits for them, and re-layouts  3.66 us (3%)
    pallas_call x1, Pallas kernels, body(): pl.pallas_call(functools.partial(kernel, shards, subs, cores, cap), out_s...  118 us
    unnamed x7, local copies, waits for them, and re-layouts  3.66 us

profile of v1, /device:TPU:14, one launch (start us, length us, event | category | flops | bytes accessed | tf_op | source)
XLA Modules:
  0.0 121.8 jit_solution(7227902709855907007)
XLA Ops:
  0.0 0.0 copy-start
  0.0 0.7 copy-done
  0.7 0.0 copy-start.1
  0.7 0.7 copy-done.1
  1.3 0.0 copy-start.2
  1.3 0.7 copy-done.2
  2.0 118.1 %shard_map.46 = f32[1024,768]{1,0:T(8,128)S(1)} custom-call(f32[1024,768]{1,0:T(8,128)} %emb.1, s32[1,1024]{1,0:T(1,128)S(1)} %bitcast.3, s32[1,4]{1,0:T(1,128)S(1)} %copy-done.1, s32[1,4]{1,0:T(1,128)S(1)} %copy-done.2), custom_call_target="tpu_custom_call" | custom-call | flops 16106127360 | bytes 6291456 | tf_op jit(solution)/shard_map/pallas_call | solution.py:246
  120.2 1.7 %copy.6 = f32[1,1024,768]{2,1,0:T(8,128)} copy(f32[1,1024,768]{2,1,0:T(8,128)S(1)} %bitcast.2) | data formatting | bytes 6291456
Async XLA Ops:
  0.0 0.7 copy-start
  0.7 0.7 copy-start.1
  1.3 0.7 copy-start.2

commit v2 on v1

--- a/solution.py
+++ b/solution.py
@@ -11,6 +11,8 @@
 epsilon = 1e-06
 LOG2E = 1.4426950408889634
 MESH = pl.DeviceIdType.MESH
+KEYS = 512
+QUERIES = 256
 ROWS = 256
 
 
@@ -130,9 +132,8 @@
             data_copy(z * bands + b, z * bands + b, z, b).wait_recv()
         address = jnp.concatenate([addr_in[z * bands + b] for b in range(bands)], axis=1)
 
-        @pl.loop(0, blocks)
-        def _(block):
-            rows = pl.ds(pl.multiple_of(block * ROWS, ROWS), ROWS)
+        for block in range(blocks):
+            rows = slice(block * ROWS, (block + 1) * ROWS)
             put = lax.broadcasted_iota(jnp.int32, (ROWS, slots), 0) + block * ROWS == address
             put = jnp.where(put, 1.0, 0.0).astype(jnp.bfloat16)
             arrived = incoming[pl.ds(z * bands, bands)].reshape(slots, width)
@@ -158,19 +159,20 @@
                     scale_copy(block, 1).start()
                     near_copy(block, 1).start()
 
-    def add_keys(keys, key_scale, key_weight, first_key, first):
-        @pl.loop(0, blocks)
-        def _(block):
-            rows = pl.ds(pl.multiple_of(block * ROWS, ROWS), ROWS)
-            gram = dot_t(own[rows], keys)
+    def add_keys(keys, key_scale, key_weight, first):
+        for start in range(0, tile, QUERIES):
+            rows = slice(start, start + QUERIES)
+            gram = dot_t(own[rows], keys[...])
             weight = jnp.exp2(
                 gram * (scale_col[rows, 0:1] * (beta * LOG2E / width)) * key_scale
             ) * key_weight
-            if first_key is not None:
-                at = lax.broadcasted_iota(jnp.int32, weight.shape, 0) + block * ROWS
-                key = lax.broadcasted_iota(jnp.int32, weight.shape, 1) + first_key
+            if first:
+                at = lax.broadcasted_iota(jnp.int32, weight.shape, 0) + start
+                key = lax.broadcasted_iota(jnp.int32, weight.shape, 1)
                 weight = jnp.where(at == key, 0.0, weight)
-            numer = jnp.dot(weight.astype(jnp.bfloat16), keys, preferred_element_type=jnp.float32)
+            numer = jnp.dot(
+                weight.astype(jnp.bfloat16), keys[...], preferred_element_type=jnp.float32
+            )
             total = weight[:, 0:128]
             for k in range(128, weight.shape[1], 128):
                 total = total + weight[:, k : k + 128]
@@ -181,34 +183,33 @@
                 acc[rows] += numer
                 denom[rows] += total
 
-    lane = lax.broadcasted_iota(jnp.int32, (1, ROWS), 1)
-
-    def counted(block, count):
-        return jnp.where(lane + block * ROWS < count, 1.0, 0.0)
+    def scales(ref, first, last):
+        return jnp.concatenate([ref[block] for block in range(first, last)], axis=1)
+
+    def counted(start, keys, count):
+        lane = lax.broadcasted_iota(jnp.int32, (1, keys), 1) + start
+        return jnp.where(lane < count, 1.0, 0.0)
 
     own_count = counts[0, shard]
-    for block in range(blocks):
-        add_keys(
-            own[block * ROWS : (block + 1) * ROWS], scale_row[block], counted(block, own_count),
-            block * ROWS, block == 0,
-        )
+    add_keys(own, scales(scale_row, 0, blocks), counted(0, tile, own_count), True)
 
     before, after = (shard + shards - 1) % shards, (shard + 1) % shards
     sides = (
         (shard > 0, counts[0, before], masks[0, before]),
         (shard < shards - 1, counts[0, after], masks[0, shard]),
     )
-    for block in range(blocks):
+    for start in range(0, tile, KEYS):
         for side, (there, count, live) in enumerate(sides):
 
             @pl.when(there)
             def _():
-                scale_copy(block, side).wait_recv()
-                near_copy(block, side).wait_recv()
-                gate = counted(block, jnp.where(live == 1, count, 0))
+                first, last = start // ROWS, (start + KEYS) // ROWS
+                for block in range(first, last):
+                    scale_copy(block, side).wait_recv()
+                    near_copy(block, side).wait_recv()
                 add_keys(
-                    near[side, block * ROWS : (block + 1) * ROWS], near_scale[side, block], gate,
-                    None, False,
+                    near.at[side, start : start + KEYS], scales(near_scale.at[side], first, last),
+                    counted(start, KEYS, jnp.where(live == 1, count, 0)), False,
                 )
 
     @pl.loop(0, blocks)

time: 123 us -> 122 us (level)
    pallas_call x1, Pallas kernels: 118 us -> 117 us  [body(): pl.pallas_call(functools.partial(kernel, shards, subs, cores, cap), out_s...]
where the time goes in v2:
time: 122 us; the launch traced here: 120 us
  Pallas kernels  117 us (96%)
  local copies, waits for them, and re-layouts  3.66 us (3%)
    pallas_call x1, Pallas kernels, body(): pl.pallas_call(functools.partial(kernel, shards, subs, cores, cap), out_s...  117 us
    unnamed x7, local copies, waits for them, and re-layouts  3.66 us

profile of v2, /device:TPU:14, one launch (start us, length us, event | category | flops | bytes accessed | tf_op | source)
XLA Modules:
  0.0 120.4 jit_solution(117160783590550599)
XLA Ops:
  0.0 0.0 copy-start
  0.0 0.7 copy-done
  0.7 0.0 copy-start.1
  0.7 0.7 copy-done.1
  1.3 0.0 copy-start.2
  1.3 0.7 copy-done.2
  2.0 116.7 %shard_map.46 = f32[1024,768]{1,0:T(8,128)S(1)} custom-call(f32[1024,768]{1,0:T(8,128)} %emb.1, s32[1,1024]{1,0:T(1,128)S(1)} %bitcast.3, s32[1,4]{1,0:T(1,128)S(1)} %copy-done.1, s32[1,4]{1,0:T(1,128)S(1)} %copy-done.2), custom_call_target="tpu_custom_call" | custom-call | flops 16106127360 | bytes 6291456 | tf_op jit(solution)/shard_map/pallas_call | solution.py:247
  118.7 1.7 %copy.6 = f32[1,1024,768]{2,1,0:T(8,128)} copy(f32[1,1024,768]{2,1,0:T(8,128)S(1)} %bitcast.2) | data formatting | bytes 6291456
Async XLA Ops:
  0.0 0.7 copy-start
  0.7 0.7 copy-start.1
  1.3 0.7 copy-start.2

commit v3 on v2

--- a/solution.py
+++ b/solution.py
@@ -11,7 +11,6 @@
 epsilon = 1e-06
 LOG2E = 1.4426950408889634
 MESH = pl.DeviceIdType.MESH
-KEYS = 512
 QUERIES = 256
 ROWS = 256
 
@@ -26,12 +25,12 @@
 
 def kernel(
     shards, subs, cores, cap,
-    emb, pos, counts, masks, out,
-    low, outgoing, incoming, addr_out, addr_in, acc, own, scale_col, scale_row, near, near_scale,
+    emb_in, pos_in, counts_in, masks_in, out,
+    emb, pos, counts, masks, loads, low, outgoing, incoming, addr_out, addr_in, acc, own, scale_col, scale_row, near, near_scale,
     denom,
     send, recv, addr_send, addr_recv, near_send, near_recv, ns_send, ns_recv,
 ):
-    tile, width = emb.shape
+    tile, width = emb_in.shape
     bands = subs * cores
     owners = shards * bands
     blocks = tile // ROWS
@@ -44,6 +43,13 @@
     def place(z, b):
         return (group, z, b // cores, b % cores)
 
+    placing = pltpu.make_async_copy(pos_in, pos, loads.at[0])
+    rows_in = pltpu.make_async_copy(emb_in, emb, loads.at[1])
+    counting = pltpu.make_async_copy(counts_in, counts, loads.at[2])
+    masking = pltpu.make_async_copy(masks_in, masks, loads.at[3])
+    for load in (placing, rows_in, counting, masking):
+        load.start()
+
     barrier = pltpu.get_barrier_semaphore()
 
     @pl.loop(1, owners)
@@ -53,7 +59,7 @@
             barrier, inc=1, device_id=place(peer // bands, peer % bands), device_id_type=MESH
         )
 
-    low[...] = emb[...].astype(jnp.bfloat16)
+    placing.wait()
     where = pos[...]
     owner = where // tile % shards * bands + where // (shards * tile)
     row = where % tile + 1
@@ -86,6 +92,8 @@
             device_id=place(z, b), device_id_type=MESH,
         )
 
+    rows_in.wait()
+    low[...] = emb[...].astype(jnp.bfloat16)
     order = far_first(shards)
     for step, dz in enumerate(order):
         z = (shard + dz) % shards
@@ -124,7 +132,7 @@
             device_id=place(z, band), device_id_type=MESH,
         )
 
-    for step, dz in enumerate(order):
+    for step, dz in enumerate([0] + [d for d in order if d != 0]):
         z = (shard + shards - dz) % shards
         for j in range(1 if dz == 0 else 0, bands):
             b = (band + bands - j) % bands
@@ -190,6 +198,8 @@
         lane = lax.broadcasted_iota(jnp.int32, (1, keys), 1) + start
         return jnp.where(lane < count, 1.0, 0.0)
 
+    counting.wait()
+    masking.wait()
     own_count = counts[0, shard]
     add_keys(own, scales(scale_row, 0, blocks), counted(0, tile, own_count), True)
 
@@ -198,23 +208,24 @@
         (shard > 0, counts[0, before], masks[0, before]),
         (shard < shards - 1, counts[0, after], masks[0, shard]),
     )
-    for start in range(0, tile, KEYS):
+    half = tile // 2
+    pieces = [(0, half)] + [(start, ROWS) for start in range(half, tile, ROWS)]
+    for start, size in pieces:
         for side, (there, count, live) in enumerate(sides):
 
             @pl.when(there)
             def _():
-                first, last = start // ROWS, (start + KEYS) // ROWS
+                first, last = start // ROWS, (start + size) // ROWS
                 for block in range(first, last):
                     scale_copy(block, side).wait_recv()
                     near_copy(block, side).wait_recv()
                 add_keys(
-                    near.at[side, start : start + KEYS], scales(near_scale.at[side], first, last),
-                    counted(start, KEYS, jnp.where(live == 1, count, 0)), False,
+                    near.at[side, start : start + size], scales(near_scale.at[side], first, last),
+                    counted(start, size, jnp.where(live == 1, count, 0)), False,
                 )
 
-    @pl.loop(0, blocks)
-    def _(block):
-        rows = pl.ds(pl.multiple_of(block * ROWS, ROWS), ROWS)
+    for block in range(blocks):
+        rows = slice(block * ROWS, (block + 1) * ROWS)
         total = jnp.sum(denom[rows], axis=1, keepdims=True)
         valid = lax.broadcasted_iota(jnp.int32, (ROWS, 1), 0) + block * ROWS < own_count
         out[rows] = jnp.where(valid, acc[rows] / total, 0.0)
@@ -241,15 +252,20 @@
     cap = 2 * tile // owners
     blocks = tile // ROWS
     vmem = pl.BlockSpec(memory_space=pltpu.VMEM)
-    smem = pl.BlockSpec(memory_space=pltpu.SMEM)
+    hbm = pl.BlockSpec(memory_space=pltpu.HBM)
     dma = pltpu.SemaphoreType.DMA
     bf16, f32 = jnp.bfloat16, jnp.float32
     result = pl.pallas_call(
         functools.partial(kernel, shards, subs, cores, cap),
         out_shape=jax.ShapeDtypeStruct((tile, width), f32),
-        in_specs=[vmem, vmem, smem, smem],
+        in_specs=[hbm, hbm, hbm, hbm],
         out_specs=vmem,
         scratch_shapes=[
+            pltpu.VMEM((tile, width), f32),
+            pltpu.VMEM((1, tile), jnp.int32),
+            pltpu.SMEM(tile_valid.shape, jnp.int32),
+            pltpu.SMEM(pair_mask.shape, jnp.int32),
+            dma((4,)),
             pltpu.VMEM((tile, width), bf16),
             pltpu.VMEM((owners, cap, width), bf16),
             pltpu.VMEM((owners, cap, width), bf16),

time: 122 us -> 118 us (0.967)
  Pallas kernels: 117 us -> 113 us
    pallas_call x1, Pallas kernels: 117 us -> 113 us  [body(): pl.pallas_call(functools.partial(kernel, shards, subs, cores, cap), out_s...]
where the time goes in v3:
time: 118 us; the launch traced here: 116 us
  Pallas kernels  113 us (96%)
  local copies, waits for them, and re-layouts  3.66 us (3%)
    pallas_call x1, Pallas kernels, body(): pl.pallas_call(functools.partial(kernel, shards, subs, cores, cap), out_s...  113 us
    unnamed x7, local copies, waits for them, and re-layouts  3.66 us

profile of v3, /device:TPU:14, one launch (start us, length us, event | category | flops | bytes accessed | tf_op | source)
XLA Modules:
  0.0 116.3 jit_solution(14742203739406491970)
XLA Ops:
  0.0 0.0 copy-start
  0.0 0.7 copy-done
  0.7 0.0 copy-start.1
  0.7 0.7 copy-done.1
  1.3 0.0 copy-start.2
  1.3 0.7 copy-done.2
  2.0 112.6 %shard_map.46 = f32[1024,768]{1,0:T(8,128)S(1)} custom-call(f32[1024,768]{1,0:T(8,128)} %emb_in.1, s32[1,1024]{1,0:T(1,128)S(1)} %bitcast.3, s32[1,4]{1,0:T(1,128)S(1)} %copy-done.1, s32[1,4]{1,0:T(1,128)S(1)} %copy-done.2), custom_call_target="tpu_custom_call" | custom-call | flops 16106127360 | bytes 6291456 | tf_op jit(solution)/shard_map/pallas_call | solution.py:258
  114.6 1.7 %copy.6 = f32[1,1024,768]{2,1,0:T(8,128)} copy(f32[1,1024,768]{2,1,0:T(8,128)S(1)} %bitcast.2) | data formatting | bytes 6291456
Async XLA Ops:
  0.0 0.7 copy-start
  0.7 0.7 copy-start.1
  1.3 0.7 copy-start.2

commit v4 on v3

--- a/solution.py
+++ b/solution.py
@@ -64,14 +64,24 @@
     owner = where // tile % shards * bands + where // (shards * tile)
     row = where % tile + 1
     chosen = lax.broadcasted_iota(jnp.int32, (owners, tile), 0) == owner
-    upto = lax.broadcasted_iota(jnp.int32, (tile, tile), 0) <= lax.broadcasted_iota(
-        jnp.int32, (tile, tile), 1
-    )
-    rank = jnp.dot(
-        jnp.where(chosen, 1.0, 0.0).astype(jnp.bfloat16),
+    upto = lax.broadcasted_iota(jnp.int32, (128, 128), 0) <= lax.broadcasted_iota(
+        jnp.int32, (128, 128), 1
+    )
+    ones = jnp.where(chosen, 1.0, 0.0)
+    runs = jnp.dot(
+        jnp.concatenate([ones[:, k : k + 128] for k in range(0, tile, 128)], axis=0).astype(
+            jnp.bfloat16
+        ),
         jnp.where(upto, 1.0, 0.0).astype(jnp.bfloat16),
         preferred_element_type=jnp.float32,
     )
+    before_run = jnp.zeros((owners, 1), jnp.float32)
+    ranks = []
+    for k in range(tile // 128):
+        run = runs[k * owners : (k + 1) * owners]
+        ranks.append(run + before_run)
+        before_run = before_run + run[:, 127:128]
+    rank = jnp.concatenate(ranks, axis=1)
     rank = jnp.sum(jnp.where(chosen, rank, 0.0), axis=0, keepdims=True).astype(jnp.int32) - 1
     slot = owner * cap + rank
     which = lax.broadcasted_iota(jnp.int32, (16, tile), 0)

time: 118 us -> 118 us (level)
  no operation moved by 1% of the time
where the time goes in v4:
time: 118 us; the launch traced here: 116 us
  Pallas kernels  113 us (96%)
  local copies, waits for them, and re-layouts  3.66 us (3%)
    pallas_call x1, Pallas kernels, body(): pl.pallas_call(functools.partial(kernel, shards, subs, cores, cap), out_s...  113 us
    unnamed x7, local copies, waits for them, and re-layouts  3.66 us

profile of v4, /device:TPU:14, one launch (start us, length us, event | category | flops | bytes accessed | tf_op | source)
XLA Modules:
  0.0 116.2 jit_solution(5399575463878428721)
XLA Ops:
  0.0 0.0 copy-start
  0.0 0.7 copy-done
  0.7 0.0 copy-start.1
  0.7 0.7 copy-done.1
  1.3 0.0 copy-start.2
  1.3 0.7 copy-done.2
  2.0 112.5 %shard_map.46 = f32[1024,768]{1,0:T(8,128)S(1)} custom-call(f32[1024,768]{1,0:T(8,128)} %emb_in.1, s32[1,1024]{1,0:T(1,128)S(1)} %bitcast.3, s32[1,4]{1,0:T(1,128)S(1)} %copy-done.1, s32[1,4]{1,0:T(1,128)S(1)} %copy-done.2), custom_call_target="tpu_custom_call" | custom-call | flops 16106127360 | bytes 6291456 | tf_op jit(solution)/shard_map/pallas_call | solution.py:268
  114.6 1.7 %copy.6 = f32[1,1024,768]{2,1,0:T(8,128)} copy(f32[1,1024,768]{2,1,0:T(8,128)S(1)} %bitcast.2) | data formatting | bytes 6291456
Async XLA Ops:
  0.0 0.7 copy-start
  0.7 0.7 copy-start.1
  1.3 0.7 copy-start.2
